TPU v7x, 256 devices: a whole 4x4x8 slice. The times are simulated.
256 devices in a mesh: seq: 128 (over y, x, z), pair: 2 (over core).
Axes of the slice: x: 4, y: 4, z: 8, core: 2. Of those that a mesh axis runs over, the one named last changes fastest.
Arguments:
- tokens_in: bfloat16 [32768, 1024], P(('seq', 'pair')), may hold values from -24 to 24
- queries: bfloat16 [32768, 1024], P(('seq', 'pair')), may hold values from -500 to 500
- key_value: bfloat16 [32768, 128], P(('seq', 'pair')), may hold values from -6 to 6
- out_grad: bfloat16 [32768, 1024], P(('seq', 'pair')), may hold values from -1.25 to 1.25
- cluster_of: int32 [32768, 16], P(('seq', 'pair')), may hold values from 0 to 1023, as said below
- slot_of: int32 [32768, 16], P(('seq', 'pair')), may hold values from 0 to 1023, as said below
Outputs:
- weight_grad: float32 [1024, 1024], P(('seq', 'pair'))
Inputs may be any that keep to these rules, and one draw needn't show every extreme that they name: `cluster_of`: cluster c belongs to owner group c // 8. Of the 2048 rows of one aligned block of 128 tokens, at most 32 name clusters of one owner group; in every draw some owner group receives exactly 32 rows from every block of even index and some from every block of odd index. No two rows share a cluster and a slot. Rows of the k-th aligned block of 128 tokens take slots of half k % 2, that is slot_of // 512 == k % 2. Half of all slots have a member in all; single clusters hold more or fewer.
All inputs are finite; a program needn't handle non-finite values.
Results may differ from a plain program's by a relative error of at most 0.0041.
Values may be sent and summed in bfloat16 or wider, within the bound.
A program may use at most 64 MiB of HBM per device.

v0:
```python
import jax
import jax.numpy as jnp
from jax import lax
from jax.sharding import PartitionSpec as P

H = 16
HD = 64
HALF = 512
CL_DEV = 8


def cluster_grad(query_part, key_part, live_keys):
    score_scale = HD ** (-0.5)
    query_rows = query_part[:, :HD]
    grad_rows = query_part[:, HD:]
    key_rows = key_part[:, :HD]
    value_rows = key_part[:, HD:]
    scores = jnp.dot(query_rows, key_rows.T, preferred_element_type=jnp.float32) * score_scale
    scores = jnp.where(live_keys[None, :] > 0, scores, jnp.float32(-1e30))
    row_max = jnp.max(scores, axis=1, keepdims=True)
    weights = jnp.exp(scores - row_max)
    probs = weights / jnp.sum(weights, axis=1, keepdims=True)
    prob_grad = jnp.dot(grad_rows, value_rows.T, preferred_element_type=jnp.float32)
    row_dot = jnp.sum(probs * prob_grad, axis=1, keepdims=True)
    score_grad = (probs * (prob_grad - row_dot) * score_scale).astype(jnp.bfloat16)
    return jnp.dot(score_grad, key_rows, preferred_element_type=jnp.float32).astype(jnp.bfloat16)


def on_device(tokens_in, queries, key_value, out_grad, cluster_of, slot_of):
    groups = lax.axis_size("seq")
    tok_count = queries.shape[0]
    row_count = tok_count * H
    bound_rows = 2 * row_count // groups
    slot_count = CL_DEV * HALF
    owners = (cluster_of // CL_DEV).reshape(row_count)
    local_slot = (cluster_of % CL_DEV * HALF + slot_of % HALF).reshape(row_count)
    picked = (owners[:, None] == jnp.arange(groups, dtype=jnp.int32)[None, :]).astype(jnp.int32)
    ranked = jnp.sum(jnp.cumsum(picked, axis=0) * picked, axis=1) - 1
    cell_index = owners * bound_rows + ranked
    paired_rows = jnp.concatenate(
        [queries.reshape(row_count, HD), out_grad.reshape(row_count, HD)], axis=1
    )
    packed = jnp.concatenate([paired_rows, jnp.repeat(key_value, H, axis=0)], axis=1)
    outgoing = jnp.zeros((groups * bound_rows, 4 * HD), jnp.bfloat16).at[cell_index].set(packed)
    labels = jnp.full((groups * bound_rows,), -1, jnp.int32).at[cell_index].set(local_slot)
    incoming, labels_in = (
        lax.all_to_all(
            outgoing.reshape(groups, bound_rows, 4 * HD),
            "seq",
            split_axis=0,
            concat_axis=0,
            tiled=True,
        ),
        lax.all_to_all(
            labels.reshape(groups, bound_rows), "seq", split_axis=0, concat_axis=0, tiled=True
        ),
    )
    target = labels_in.reshape(groups * bound_rows)
    target_safe = jnp.where(target >= 0, target, slot_count)
    arranged = (
        jnp.zeros((slot_count, 4 * HD), jnp.bfloat16)
        .at[target_safe]
        .set(incoming.reshape(groups * bound_rows, 4 * HD), mode="drop")
    )
    live_slot = (
        jnp.zeros((slot_count,), jnp.bfloat16)
        .at[target_safe]
        .set(jnp.ones((groups * bound_rows,), jnp.bfloat16), mode="drop")
    )
    arranged = arranged.reshape(CL_DEV, HALF, 4 * HD)
    keys_all, live_all = (
        lax.all_gather(arranged[:, :, 2 * HD :], "pair", axis=1, tiled=True),
        lax.all_gather(live_slot.reshape(CL_DEV, HALF), "pair", axis=1, tiled=True),
    )

    def per_cluster(operands):
        return cluster_grad(operands[0], operands[1], operands[2])

    cluster_grads = lax.map(per_cluster, (arranged[:, :, : 2 * HD], keys_all, live_all))
    slot_grads = cluster_grads.reshape(slot_count, HD)
    going_back = jnp.where(
        target[:, None] >= 0,
        slot_grads[jnp.minimum(target_safe, slot_count - 1)],
        jnp.zeros((), jnp.bfloat16),
    )
    returned = lax.all_to_all(
        going_back.reshape(groups, bound_rows // 2, 2 * HD),
        "seq",
        split_axis=0,
        concat_axis=0,
        tiled=True,
    )
    query_grad = returned.reshape(groups * bound_rows, HD)[cell_index].reshape(tok_count, H * HD)
    return lax.psum_scatter(
        lax.dot_general(
            tokens_in, query_grad, (((0,), (0,)), ((), ())), preferred_element_type=jnp.float32
        ),
        ("seq", "pair"),
        scatter_dimension=0,
        tiled=True,
    )


def solution(mesh):
    return jax.shard_map(
        on_device,
        mesh=mesh,
        in_specs=(
            P(("seq", "pair"), None),
            P(("seq", "pair"), None),
            P(("seq", "pair"), None),
            P(("seq", "pair"), None),
            P(("seq", "pair"), None),
            P(("seq", "pair"), None),
        ),
        out_specs=P(("seq", "pair"), None),
        check_vma=False,
    )
```

profile of v0, /device:TPU:2, one launch (start us, length us, event | category | flops | bytes accessed | tf_op | source)
XLA Modules:
  0.0 521.5 jit_solution(5490226799188540222)
XLA Ops:
  6.5 0.8 broadcast_multiply_fusion
  8.9 0.6 fusion.22
  9.6 8.1 %scatter_custom_fusion = s32[4096]{0:T(1024)S(1)} fusion(s32[2048]{0:T(1024)S(1)} %bitcast.51, s32[2048]{0:T(1024)S(1)} %reshape.186, s32[]{:T(128)} %constant.76.clone.1), kind=kCustom, calls=%fused_computation.67 | custom fusion | bytes 16388 | tf_op jit(solution)/shard_map/scatter | solution.py:45
  17.7 0.7 all_to_all.12
  18.4 15.4 %all-to-all-start = ((s32[128,1,32]{2,1,0:T(1,128)}), s32[128,1,32]{2,1,0:T(1,128)S(1)}, u32[]{:S(2)}, u32[]{:S(2)}) async-start(s32[128,1,32]{2,1,0:T(1,128)} %bitcast.8), calls=%async_computation | async-start | bytes 131072 | tf_op jit(solution)/shard_map/all_to_all | solution.py:54
  34.6 11.5 %scatter_custom_fusion.2 = bf16[4096,256]{1,0:T(8,128)(2,1)} fusion(s32[2048]{0:T(1024)S(1)} %bitcast.52, bf16[2048,128]{1,0:T(8,128)(2,1)S(1)} %bitcast.49, bf16[]{:T(256)} %constant.101, bf16[2048,64]{1,0:T(8,128)(2,1)S(1)} %reshape.158, bf16[2048,64]{1,0:T(8,128)(2,1)S(1)} %reshape.157, bf16[]{:T(256)} %constant.86.clone.1), kind=kCustom, calls=%fused_computation.30 | custom fusion | flops 3145728 | bytes 3670020 | tf_op jit(solution)/shard_map/scatter | solution.py:44
  46.2 13.8 %all-to-all-start.1 = ((bf16[128,32,256]{2,1,0:T(8,128)(2,1)}), bf16[128,32,256]{2,1,0:T(8,128)(2,1)S(1)}, u32[]{:S(2)}, u32[]{:S(2)}) async-start(bf16[128,32,256]{2,1,0:T(8,128)(2,1)} %bitcast.12), calls=%async_computation.1 | async-start | bytes 4194304 | tf_op jit(solution)/shard_map/all_to_all | solution.py:47
  60.7 0.8 reduce.5
  61.7 49.1 %all-to-all-done.1 = bf16[128,32,256]{2,1,0:T(8,128)(2,1)S(1)} async-done(((bf16[128,32,256]{2,1,0:T(8,128)(2,1)}), bf16[128,32,256]{2,1,0:T(8,128)(2,1)S(1)}, u32[]{:S(2)}, u32[]{:S(2)}) %all-to-all-start.1) | async-done | bytes 2097184 | tf_op jit(solution)/shard_map/all_to_all | solution.py:47
  110.8 1.3 copy-done.1
  112.1 18.9 %scatter_custom_fusion.3 = bf16[4096,256]{1,0:T(8,128)(2,1)S(1)} fusion(s32[4096]{0:T(1024)S(1)} %bitcast.55, bf16[4096,256]{1,0:T(8,128)(2,1)} %bitcast.48, bf16[]{:T(256)} %constant.86.clone.1), kind=kCustom, calls=%fused_computation.38 | custom fusion | bytes 2097664 | tf_op jit(solution)/shard_map/scatter | solution.py:63
  131.0 1.5 fusion.38
  132.7 28.6 %scatter_custom_fusion.1 = bf16[4096]{0:T(1024)(128)(2,1)S(1)} fusion(s32[4096]{0:T(1024)S(1)} %bitcast.56, bf16[4096]{0:T(1024)(128)(2,1)S(1)} %broadcast.158, bf16[]{:T(256)} %constant.86.clone.1), kind=kCustom, calls=%fused_computation.72 | custom fusion | bytes 8194 | tf_op jit(solution)/shard_map/scatter | solution.py:68
  161.3 2.0 all_gather.6
  163.3 32.5 %while.10 = (s32[]{:T(128)}, bf16[8,512,64]{1,2,0:T(8,128)(2,1)S(1)}, bf16[8,1024]{1,0:T(8,128)(2,1)S(1)}, bf16[8,512,128]{2,1,0:T(8,128)(2,1)S(1)}, bf16[8,1024,128]{2,1,0:T(8,128)(2,1)}, /*index=5*/s32[]{:T(128)}) while((s32[]{:T(128)}, bf16[8,512,64]{1,2,0:T(8,128)(2,1)S(1)}, bf16[8,1024]{1,0:T(8,128)(2,1)S(1)}, ...), condition=%wide.region_11.12_spmd, body=%wide.region_7.11_spmd.sunk | while | flops 212370944 | bytes 14509149 | solution.py:79
  163.4 1.0 dynamic-slice_bitcast_fusion.4
  164.4 0.5 fusion.46
  164.9 0.6 fusion.47
  165.5 0.9 multiply_reduce_fusion.2
  166.4 1.0 fusion.48
  167.5 1.0 dynamic-slice_bitcast_fusion.4
  168.4 0.5 fusion.46
  169.0 0.6 fusion.47
  169.5 0.9 multiply_reduce_fusion.2
  170.4 1.0 fusion.48
  171.5 1.0 dynamic-slice_bitcast_fusion.4
  172.5 0.5 fusion.46
  173.0 0.6 fusion.47
  173.6 0.9 multiply_reduce_fusion.2
  174.5 1.0 fusion.48
  175.6 1.0 dynamic-slice_bitcast_fusion.4
  176.6 0.5 fusion.46
  177.1 0.6 fusion.47
  177.7 0.9 multiply_reduce_fusion.2
  178.5 1.0 fusion.48
  179.6 1.0 dynamic-slice_bitcast_fusion.4
  180.6 0.5 fusion.46
  181.1 0.6 fusion.47
  181.7 0.9 multiply_reduce_fusion.2
  182.6 1.0 fusion.48
  183.7 1.0 dynamic-slice_bitcast_fusion.4
  184.7 0.5 fusion.46
  185.2 0.6 fusion.47
  185.8 0.9 multiply_reduce_fusion.2
  186.7 1.0 fusion.48
  187.8 1.0 dynamic-slice_bitcast_fusion.4
  188.7 0.5 fusion.46
  189.3 0.6 fusion.47
  189.8 0.9 multiply_reduce_fusion.2
  190.7 1.0 fusion.48
  191.8 1.0 dynamic-slice_bitcast_fusion.4
  192.8 0.5 fusion.46
  193.3 0.6 fusion.47
  193.9 0.9 multiply_reduce_fusion.2
  194.8 1.0 fusion.48
  196.3 12.1 %gather_fusion = bf16[4096,64]{1,0:T(8,128)(2,1)S(1)} fusion(bf16[4096,64]{1,0:T(8,128)(2,1)S(1)} %bitcast.46, s32[4096]{0:T(1024)S(1)} %broadcast_clamp_fusion), kind=kCustom, calls=%fused_computation | custom fusion | bytes 1064960 | tf_op jit(solution)/shard_map/gather | solution.py:83
  209.5 1.2 copy.42
  210.6 9.1 %all-to-all-start.2 = ((bf16[128,16,128]{2,1,0:T(8,128)(2,1)}), bf16[128,16,128]{2,1,0:T(8,128)(2,1)S(1)}, u32[]{:S(2)}, u32[]{:S(2)}) async-start(bf16[128,16,128]{2,1,0:T(8,128)(2,1)} %copy.42), calls=%async_computation.2 | async-start | bytes 1048576 | tf_op jit(solution)/shard_map/all_to_all | solution.py:86
  219.8 18.6 %all-to-all-done.2 = bf16[128,16,128]{2,1,0:T(8,128)(2,1)S(1)} async-done(((bf16[128,16,128]{2,1,0:T(8,128)(2,1)}), bf16[128,16,128]{2,1,0:T(8,128)(2,1)S(1)}, u32[]{:S(2)}, u32[]{:S(2)}) %all-to-all-start.2) | async-done | bytes 524320 | tf_op jit(solution)/shard_map/all_to_all | solution.py:86
  238.8 6.2 %gather_fusion.1 = bf16[2048,64]{1,0:T(8,128)(2,1)S(1)} fusion(bf16[4096,64]{1,0:T(8,128)(2,1)S(1)} %reshape.164, s32[2048]{0:T(1024)S(1)} %broadcast_clamp_fusion.1), kind=kCustom, calls=%fused_computation.1 | custom fusion | bytes 532480 | tf_op jit(solution)/shard_map/gather | solution.py:93
  245.4 2.7 convolution_bitcast_fusion
  248.1 264.6 %all-reduce.3.cloned.1.call-done = f32[1024,1024]{0,1:T(8,128)} async-done(((f32[1024,1024]{0,1:T(8,128)}), f32[1024,1024]{0,1:T(8,128)}) %all-reduce.3.cloned.1.call-update) | async-done | bytes 4194320
  512.7 1.2 constant_dynamic-slice_fusion
  513.9 0.8 copy.43
  (67 shorter events, 6.0 us)
Async XLA Ops:
  6.5 238.8 %copy-start = (bf16[128,1024]{1,0:T(8,128)(2,1)S(1)}, bf16[128,1024]{1,0:T(8,128)(2,1)}, u32[]{:S(2)}) copy-start(bf16[128,1024]{1,0:T(8,128)(2,1)} %param.8) | copy-start | bytes 786436
  8.5 25.3 %copy-start.2 = (bf16[128,1024]{1,0:T(8,128)(2,1)S(1)}, bf16[128,1024]{1,0:T(8,128)(2,1)}, u32[]{:S(2)}) copy-start(bf16[128,1024]{1,0:T(8,128)(2,1)} %param.9) | copy-start | bytes 786436
  8.6 25.6 %copy-start.3 = (bf16[128,1024]{1,0:T(8,128)(2,1)S(1)}, bf16[128,1024]{1,0:T(8,128)(2,1)}, u32[]{:S(2)}) copy-start(bf16[128,1024]{1,0:T(8,128)(2,1)} %param.11) | copy-start | bytes 786436
  8.6 26.0 %copy-start.4 = (bf16[128,128]{1,0:T(8,128)(2,1)S(1)}, bf16[128,128]{1,0:T(8,128)(2,1)}, u32[]{:S(2)}) copy-start(bf16[128,128]{1,0:T(8,128)(2,1)} %param.10) | copy-start | bytes 98308
  18.4 27.8 %all-to-all-start = ((s32[128,1,32]{2,1,0:T(1,128)}), s32[128,1,32]{2,1,0:T(1,128)S(1)}, u32[]{:S(2)}, u32[]{:S(2)}) async-start(s32[128,1,32]{2,1,0:T(1,128)} %bitcast.8), calls=%async_computation | async-start | bytes 131072 | tf_op jit(solution)/shard_map/all_to_all | solution.py:54
  46.2 64.6 %all-to-all-start.1 = ((bf16[128,32,256]{2,1,0:T(8,128)(2,1)}), bf16[128,32,256]{2,1,0:T(8,128)(2,1)S(1)}, u32[]{:S(2)}, u32[]{:S(2)}) async-start(bf16[128,32,256]{2,1,0:T(8,128)(2,1)} %bitcast.12), calls=%async_computation.1 | async-start | bytes 4194304 | tf_op jit(solution)/shard_map/all_to_all | solution.py:47
  60.0 103.4 %all-gather.2.cloned.1.call-start = ((), (), s32[]{:S(2)}) async-start(), calls=%async_computation.3 | async-start | bytes 3145728 | tf_op jit(solution)/shard_map/all_gather | solution.py:72
  110.8 1.4 copy-start.1
  210.6 27.8 %all-to-all-start.2 = ((bf16[128,16,128]{2,1,0:T(8,128)(2,1)}), bf16[128,16,128]{2,1,0:T(8,128)(2,1)S(1)}, u32[]{:S(2)}, u32[]{:S(2)}) async-start(bf16[128,16,128]{2,1,0:T(8,128)(2,1)} %copy.42), calls=%async_computation.2 | async-start | bytes 1048576 | tf_op jit(solution)/shard_map/all_to_all | solution.py:86
  219.8 292.9 %all-reduce.3.cloned.1.call-start = ((), (), s32[]{:S(2)}) async-start(), calls=%async_computation.4 | async-start | bytes 8388608
Sparse Core Ops, SparseCore 0:
  132.7 11.6 all-gather.1
  248.2 264.3 all-reduce.2
where the time goes:
time: 522 us
  waiting for transfers between devices  332 us (64%)
  local copies, waits for them, and re-layouts  93.3 us (18%)
  starting transfers between devices  38.6 us (7%)
  matrix products  22.1 us (4%)
  other arithmetic  19.2 us (4%)
  between operations  13.7 us (3%)
    unnamed x3, waiting for transfers between devices  265 us
    all_to_all x1, waiting for transfers between devices, on_device(): lax.all_to_all(outgoing.reshape(groups, bound_rows, 4 * HD), 'seq', split...  49.1 us
    scatter x1, local copies, waits for them, and re-layouts, on_device(): live_slot = jnp.zeros((slot_count,), jnp.bfloat16).at[target_safe].set(jn...  28.6 us
    scatter x1, local copies, waits for them, and re-layouts, on_device(): arranged = jnp.zeros((slot_count, 4 * HD), jnp.bfloat16).at[target_safe]....  18.9 us
    all_to_all x1, waiting for transfers between devices, on_device(): lax.all_to_all(going_back.reshape(groups, bound_rows // 2, 2 * HD), 'seq'...  18.6 us
    all_to_all x1, starting transfers between devices, on_device(): lax.all_to_all(labels.reshape(groups, bound_rows), 'seq', split_axis=0, c...  15.4 us
    all_to_all x1, starting transfers between devices, on_device(): lax.all_to_all(outgoing.reshape(groups, bound_rows, 4 * HD), 'seq', split...  13.8 us
    gather x3, local copies, waits for them, and re-layouts, on_device(): slot_grads[jnp.minimum(target_safe, slot_count - 1)]  13.1 us
  transfers between devices with their start and end apart: 5, of which 3 were waited for; matrix products, arithmetic and copies ran while one was open for 8% of the time, Pallas kernels for 0%

commit v1 on v0

v1 whole, which is shorter than its diff:
```python
import functools

import jax
import jax.numpy as jnp
from jax import lax
from jax.experimental import pallas as pl
from jax.experimental.pallas import tpu as pltpu
from jax.sharding import PartitionSpec as P

H = 16
HD = 64
HALF = 512
CL_DEV = 8
TOK = 128
ROWS = TOK * H
SLOTS = CL_DEV * HALF
GROUPS = 128
BOUND = 32
PLANE = 16
DEPTH = 8
CHUNKS = 8
PER = GROUPS // CHUNKS
MESH = pl.DeviceIdType.MESH
F32 = jnp.float32
BF16 = jnp.bfloat16
VMEM = pl.BlockSpec(memory_space=pltpu.VMEM)


def params(collective=None):
    if collective is None:
        return pltpu.CompilerParams(vmem_limit_bytes=56 * 2**20)
    return pltpu.CompilerParams(
        vmem_limit_bytes=56 * 2**20, collective_id=collective, has_side_effects=True
    )


def iota(shape, dim):
    return lax.broadcasted_iota(jnp.int32, shape, dim)


def one_hot(mask):
    return jnp.where(mask, 1.0, 0.0).astype(BF16)


def dot(a, b):
    return jnp.dot(a, b, preferred_element_type=F32)


def dot_t(a, b):
    return lax.dot_general(a, b, (((1,), (1,)), ((), ())), preferred_element_type=F32)


def t_dot(a, b):
    return lax.dot_general(a, b, (((0,), (0,)), ((), ())), preferred_element_type=F32)


def pack_kernel(idx_ref, q_ref, g_ref, kv_ref, out_ref, lab_ref, cell_ref, rows_ref, pick_ref):
    cluster = idx_ref[0:1, :]
    slot = idx_ref[1:2, :]
    owner = lax.shift_right_logical(cluster, 3)
    local = (cluster & (CL_DEV - 1)) * HALF + (slot & (HALF - 1))
    pick_ref[...] = jnp.where(iota((GROUPS, ROWS), 0) == owner, 1.0, 0.0)
    before = one_hot(iota((TOK, TOK), 0) < iota((TOK, TOK), 1))
    base = jnp.zeros((GROUPS, 1), F32)
    ranks = []
    for h in range(H):
        pick = pick_ref[:, h * TOK : (h + 1) * TOK]
        count = dot(pick.astype(BF16), before) + base
        ranks.append(jnp.sum(pick * count, axis=0, keepdims=True))
        base = base + jnp.sum(pick, axis=1, keepdims=True)
    rank = jnp.concatenate(ranks, axis=1).astype(jnp.int32)
    cell = owner * BOUND + rank
    cell_ref[0:1, :] = cell
    at_rank = one_hot(iota((TOK, ROWS), 0) == rank)
    pick = pick_ref[...]
    high = dot_t((pick * lax.shift_right_logical(local, 6).astype(F32)).astype(BF16), at_rank)
    low = dot_t((pick * (local & 63).astype(F32)).astype(BF16), at_rank)
    live = dot_t(pick.astype(BF16), at_rank)
    label = jnp.where(live > 0.5, high * 64.0 + low, -1.0).astype(jnp.int32)
    for o in range(GROUPS):
        lab_ref[o] = label[o : o + 1, :]
    for h in range(H):
        cut = slice(h * HD, (h + 1) * HD)
        rows_ref[h * TOK : (h + 1) * TOK, :] = jnp.concatenate(
            [q_ref[:, cut], g_ref[:, cut], kv_ref[...]], axis=1
        )

    def step(c, carry):
        hot = one_hot(iota((256, ROWS), 0) == cell - c * 256)
        out_ref[pl.ds(c * 8, 8)] = dot(hot, rows_ref[...]).astype(BF16).reshape(8, BOUND, 4 * HD)
        return carry

    lax.fori_loop(0, GROUPS * BOUND // 256, step, 0)


def pack(idx, queries, out_grad, key_value):
    return pl.pallas_call(
        pack_kernel,
        out_shape=(
            jax.ShapeDtypeStruct((GROUPS, BOUND, 4 * HD), BF16),
            jax.ShapeDtypeStruct((GROUPS, 1, 128), jnp.int32),
            jax.ShapeDtypeStruct((1, ROWS), jnp.int32),
        ),
        in_specs=[VMEM] * 4,
        out_specs=(VMEM,) * 3,
        scratch_shapes=[pltpu.VMEM((ROWS, 4 * HD), BF16), pltpu.VMEM((GROUPS, ROWS), F32)],
        compiler_params=params(),
    )(idx, queries, out_grad, key_value)


def greet_all(seq, pair):
    barrier = pltpu.get_barrier_semaphore()

    def hello(i, carry):
        pl.semaphore_signal(
            barrier, inc=1, device_id=(lax.rem(seq + i, GROUPS), pair), device_id_type=MESH
        )
        return carry

    lax.fori_loop(1, GROUPS, hello, 0)
    return barrier


def forward_kernel(
    out_ref, lab_ref, qg_ref, kv_ref, live_ref, lane_ref, rows_ref, labs_ref, total_ref,
    send_sem, lsend_sem, recv_sem, lrecv_sem, own_sem,
):
    seq, pair = lax.axis_index("seq"), lax.axis_index("pair")
    barrier = greet_all(seq, pair)
    own = pltpu.make_async_copy(out_ref.at[seq], rows_ref.at[0], own_sem.at[0])
    own.start()
    own_lab = pltpu.make_async_copy(lab_ref.at[seq], labs_ref.at[0], own_sem.at[1])
    own_lab.start()
    pl.semaphore_wait(barrier, GROUPS - 1)

    def send(i, carry):
        to = lax.rem(seq + i, GROUPS)
        pltpu.make_async_remote_copy(
            src_ref=lab_ref.at[to], dst_ref=labs_ref.at[i], send_sem=lsend_sem, recv_sem=lrecv_sem,
            device_id=(to, pair), device_id_type=MESH,
        ).start()
        pltpu.make_async_remote_copy(
            src_ref=out_ref.at[to], dst_ref=rows_ref.at[i], send_sem=send_sem,
            recv_sem=recv_sem.at[i // PER], device_id=(to, pair), device_id_type=MESH,
        ).start()
        return carry

    lax.fori_loop(1, GROUPS, send, 0)
    own.wait()
    own_lab.wait()
    rest = pl.ds(1, GROUPS - 1)
    labels_done = pltpu.make_async_remote_copy(
        src_ref=lab_ref.at[rest], dst_ref=labs_ref.at[rest], send_sem=lsend_sem, recv_sem=lrecv_sem,
        device_id=(seq, pair), device_id_type=MESH,
    )
    labels_done.wait_recv()
    live = jnp.zeros((SLOTS // 128, 128), F32)
    for k in range(CHUNKS):
        lane = jnp.concatenate(
            [labs_ref[i, :, 0:BOUND] for i in range(k * PER, (k + 1) * PER)], axis=1
        )
        lane_ref[k : k + 1, :] = lane
        width = PER * BOUND
        live = live + dot_t(
            one_hot(iota((SLOTS // 128, width), 0) == lax.shift_right_arithmetic(lane, 7)),
            one_hot(iota((128, width), 0) == (lane & 127)),
        )
        part = pl.ds(max(1, k * PER), PER - (k == 0))
        pltpu.make_async_remote_copy(
            src_ref=out_ref.at[part], dst_ref=rows_ref.at[part], send_sem=send_sem,
            recv_sem=recv_sem.at[k], device_id=(seq, pair), device_id_type=MESH,
        ).wait_recv()
        rows = rows_ref[k * PER : (k + 1) * PER].reshape(width, 4 * HD)

        def add(b, carry, k=k, lane=lane, rows=rows):
            hot = one_hot(iota((HALF, width), 0) == lane - b * HALF)
            term = dot(hot, rows)
            if k == 0:
                total_ref[b] = term
            elif k < CHUNKS - 1:
                total_ref[b] += term
            else:
                done = (total_ref[b] + term).astype(BF16)
                qg_ref[b] = done[:, : 2 * HD]
                kv_ref[b] = done[:, 2 * HD :]
            return carry

        lax.fori_loop(0, CL_DEV, add, 0)
    for c in range(CL_DEV):
        live_ref[c] = live[4 * c : 4 * c + 4, :]
    labels_done.wait_send()
    pltpu.make_async_remote_copy(
        src_ref=out_ref.at[rest], dst_ref=rows_ref.at[rest], send_sem=send_sem,
        recv_sem=recv_sem.at[0], device_id=(seq, pair), device_id_type=MESH,
    ).wait_send()


def forward(outgoing, labels):
    return pl.pallas_call(
        forward_kernel,
        out_shape=(
            jax.ShapeDtypeStruct((CL_DEV, HALF, 2 * HD), BF16),
            jax.ShapeDtypeStruct((CL_DEV, HALF, 2 * HD), BF16),
            jax.ShapeDtypeStruct((CL_DEV, 4, 128), F32),
            jax.ShapeDtypeStruct((CHUNKS, PER * BOUND), jnp.int32),
        ),
        in_specs=[VMEM] * 2,
        out_specs=(VMEM,) * 4,
        scratch_shapes=[
            pltpu.VMEM((GROUPS, BOUND, 4 * HD), BF16),
            pltpu.VMEM((GROUPS, 1, 128), jnp.int32),
            pltpu.VMEM((CL_DEV, HALF, 4 * HD), F32),
            pltpu.SemaphoreType.DMA,
            pltpu.SemaphoreType.DMA,
            pltpu.SemaphoreType.DMA((CHUNKS,)),
            pltpu.SemaphoreType.DMA,
            pltpu.SemaphoreType.DMA((2,)),
        ],
        compiler_params=params(0),
    )(outgoing, labels)


def attend_kernel(
    qg_ref, kv_ref, live_ref, lane_ref, back_ref, kv2_ref, live2_ref, s_ref, d_ref, w_ref, grads_ref,
    send_sem, recv_sem,
):
    seq, pair = lax.axis_index("seq"), lax.axis_index("pair")
    other = (seq, 1 - pair)
    barrier = pltpu.get_barrier_semaphore()
    pl.semaphore_signal(barrier, inc=1, device_id=other, device_id_type=MESH)
    pl.semaphore_wait(barrier, 1)

    def copy_of(c):
        return pltpu.make_async_remote_copy(
            src_ref=kv_ref.at[c], dst_ref=kv2_ref.at[c], send_sem=send_sem.at[c],
            recv_sem=recv_sem.at[c], device_id=other, device_id_type=MESH,
        )

    live_copy = pltpu.make_async_remote_copy(
        src_ref=live_ref, dst_ref=live2_ref, send_sem=send_sem.at[CL_DEV],
        recv_sem=recv_sem.at[CL_DEV], device_id=other, device_id_type=MESH,
    )
    live_copy.start()
    for c in range(CL_DEV):
        copy_of(c).start()
    live_copy.wait()

    for c in range(CL_DEV):
        copy_of(c).wait()
        queries = qg_ref[c, :, :HD] * BF16(HD**-0.5)
        grads = qg_ref[c, :, HD:]
        keys = jnp.concatenate([kv_ref[c, :, :HD], kv2_ref[c, :, :HD]], axis=0)
        values = jnp.concatenate([kv_ref[c, :, HD:], kv2_ref[c, :, HD:]], axis=0)
        alive = jnp.concatenate(
            [ref[c, r : r + 1, :] for ref in (live_ref, live2_ref) for r in range(4)], axis=1
        )
        bias = jnp.where(alive > 0.5, 0.0, -1e30)
        s_ref[...] = dot_t(queries, keys)
        d_ref[...] = dot_t(grads, values)

        def rows(r, carry, bias=bias):
            at = pl.ds(pl.multiple_of(r * 32, 32), 32)
            scores = s_ref[at, :] + bias
            weights = jnp.exp(scores - jnp.max(scores, axis=1, keepdims=True))
            inverse = 1.0 / jnp.sum(weights, axis=1, keepdims=True)
            prob_grad = d_ref[at, :]
            row_dot = jnp.sum(weights * prob_grad, axis=1, keepdims=True) * inverse
            w_ref[at, :] = (
                weights * (prob_grad - row_dot) * (inverse * (HD**-0.5))
            ).astype(BF16)
            return carry

        lax.fori_loop(0, HALF // 32, rows, 0)
        place = slice((c % 2) * HALF, (c % 2 + 1) * HALF)
        column = slice((c // 2) * HD, (c // 2 + 1) * HD)
        grads_ref[place, column] = dot(w_ref[...], keys).astype(BF16)

    width = PER * BOUND
    for k in range(CHUNKS):
        labels = jnp.broadcast_to(lane_ref[k : k + 1, :], (128, width)).T
        low = labels & 1023
        hot = jnp.concatenate(
            [one_hot(low == iota((width, 128), 1) + 128 * b) for b in range(8)], axis=1
        )
        found = dot(hot, grads_ref[...])
        high = lax.shift_right_arithmetic(labels[:, :HD], 10)
        row = jnp.zeros((width, HD), F32)
        for a in range(4):
            row = row + jnp.where(high == a, found[:, a * HD : (a + 1) * HD], 0.0)
        row = row.reshape(PER, BOUND, HD)
        back_ref[k * PER : (k + 1) * PER] = jnp.concatenate(
            [row[:, : BOUND // 2], row[:, BOUND // 2 :]], axis=2
        ).astype(BF16)


def attend(qg, kv, live, lane):
    return pl.pallas_call(
        attend_kernel,
        out_shape=jax.ShapeDtypeStruct((GROUPS, BOUND // 2, 2 * HD), BF16),
        in_specs=[VMEM] * 4,
        out_specs=VMEM,
        scratch_shapes=[
            pltpu.VMEM((CL_DEV, HALF, 2 * HD), BF16),
            pltpu.VMEM((CL_DEV, 4, 128), F32),
            pltpu.VMEM((HALF, 2 * HALF), F32),
            pltpu.VMEM((HALF, 2 * HALF), F32),
            pltpu.VMEM((HALF, 2 * HALF), BF16),
            pltpu.VMEM((2 * HALF, 4 * HD), BF16),
            pltpu.SemaphoreType.DMA((CL_DEV + 1,)),
            pltpu.SemaphoreType.DMA((CL_DEV + 1,)),
        ],
        compiler_params=params(1),
    )(qg, kv, live, lane)


def reduce_kernel(
    back_ref, cell_ref, x_ref, out_ref, got_ref, xp_ref, g_ref, xo_ref, go_ref, part_ref, plane_ref,
    line_ref, lined_ref, send_sem, recv_sem, own_sem, psend_sem, precv_sem, ysend_sem, yrecv_sem,
    zsend_sem, zrecv_sem,
):
    seq, pair = lax.axis_index("seq"), lax.axis_index("pair")
    other = (seq, 1 - pair)
    yx, z = seq // DEPTH, lax.rem(seq, DEPTH)
    barrier = greet_all(seq, pair)
    pl.semaphore_signal(barrier, inc=1, device_id=other, device_id_type=MESH)
    own = pltpu.make_async_copy(back_ref.at[0], got_ref.at[0], own_sem)
    own.start()
    pl.semaphore_wait(barrier, GROUPS)

    def send(i, carry):
        to = lax.rem(seq + (GROUPS - i), GROUPS)
        pltpu.make_async_remote_copy(
            src_ref=back_ref.at[i], dst_ref=got_ref.at[i], send_sem=send_sem, recv_sem=recv_sem,
            device_id=(to, pair), device_id_type=MESH,
        ).start()
        return carry

    lax.fori_loop(1, GROUPS, send, 0)
    position = iota((1024, 512), 1)
    for p in range(2):
        column = lax.shift_right_logical(position, 2) * 8 + 4 * p + (position & 3)
        xp_ref[p] = dot(x_ref[...], one_hot(iota((1024, 512), 0) == column)).astype(BF16)
    x_copy = pltpu.make_async_remote_copy(
        src_ref=xp_ref.at[1 - pair], dst_ref=xo_ref, send_sem=psend_sem.at[0],
        recv_sem=precv_sem.at[0], device_id=other, device_id_type=MESH,
    )
    x_copy.start()
    own.wait()
    rest = pl.ds(1, GROUPS - 1)
    pltpu.make_async_remote_copy(
        src_ref=back_ref.at[rest], dst_ref=got_ref.at[rest], send_sem=send_sem, recv_sem=recv_sem,
        device_id=other, device_id_type=MESH,
    ).wait()
    got = got_ref[...].reshape(GROUPS * BOUND // 2, 2 * HD)
    for h in range(0, H, 2):
        pieces = []
        for e in range(2):
            cell = cell_ref[0:1, (h + e) * TOK : (h + e + 1) * TOK]
            cell = jnp.broadcast_to(cell, (TOK, TOK)).T
            offset = lax.rem(lax.shift_right_logical(cell, 5) + (GROUPS - seq), GROUPS)
            target = offset * (BOUND // 2) + (cell & (BOUND // 2 - 1))
            hot = jnp.concatenate(
                [one_hot(target == iota((TOK, 128), 1) + 128 * b) for b in range(16)], axis=1
            )
            found = dot(hot, got)
            upper = (cell[:, :HD] & (BOUND // 2)) > 0
            pieces.append(jnp.where(upper, found[:, HD:], found[:, :HD]))
        g_ref[:, h * HD : (h + 2) * HD] = jnp.concatenate(pieces, axis=1).astype(BF16)
    g_copy = pltpu.make_async_remote_copy(
        src_ref=g_ref, dst_ref=go_ref, send_sem=psend_sem.at[1], recv_sem=precv_sem.at[1],
        device_id=other, device_id_type=MESH,
    )
    g_copy.start()
    x_copy.wait()
    g_copy.wait()
    left, right = xp_ref[pair], xo_ref[...]
    for b in range(4):
        cut = slice(b * 128, (b + 1) * 128)
        term = t_dot(left[:, cut], g_ref[...]) + t_dot(right[:, cut], go_ref[...])
        part_ref[b * 4 : (b + 1) * 4] = term.astype(BF16).reshape(4, 32, 1024)

    def plane_copy(i):
        to = lax.rem(yx + i, PLANE)
        return pltpu.make_async_remote_copy(
            src_ref=part_ref.at[to], dst_ref=plane_ref.at[i - 1], send_sem=ysend_sem.at[i - 1],
            recv_sem=yrecv_sem.at[i - 1], device_id=(to * DEPTH + z, pair), device_id_type=MESH,
        )

    for i in range(1, PLANE):
        plane_copy(i).start()
    total = part_ref[yx].astype(F32)
    for i in range(1, PLANE):
        plane_copy(i).wait_recv()
        total = total + plane_ref[i - 1].astype(F32)
    for i in range(DEPTH):
        rows = total[4 * i : 4 * i + 4, :]
        line_ref[i] = jnp.concatenate([rows[:, :512], rows[:, 512:]], axis=0)

    def line_copy(i):
        to = lax.rem(z + i, DEPTH)
        return pltpu.make_async_remote_copy(
            src_ref=line_ref.at[to], dst_ref=lined_ref.at[i - 1], send_sem=zsend_sem.at[i - 1],
            recv_sem=zrecv_sem.at[i - 1], device_id=(yx * DEPTH + to, pair), device_id_type=MESH,
        )

    for i in range(1, DEPTH):
        line_copy(i).start()
    result = line_ref[z]
    for i in range(1, DEPTH):
        line_copy(i).wait_recv()
        result = result + lined_ref[i - 1]
    out_ref[...] = jnp.concatenate([result[:4], result[4:]], axis=1)
    for i in range(1, PLANE):
        plane_copy(i).wait_send()
    for i in range(1, DEPTH):
        line_copy(i).wait_send()


def reduce(back, cell, tokens_in):
    return pl.pallas_call(
        reduce_kernel,
        out_shape=jax.ShapeDtypeStruct((4, 1024), F32),
        in_specs=[VMEM] * 3,
        out_specs=VMEM,
        scratch_shapes=[
            pltpu.VMEM((GROUPS, BOUND // 2, 2 * HD), BF16),
            pltpu.VMEM((2, TOK, 512), BF16),
            pltpu.VMEM((TOK, 1024), BF16),
            pltpu.VMEM((TOK, 512), BF16),
            pltpu.VMEM((TOK, 1024), BF16),
            pltpu.VMEM((PLANE, 32, 1024), BF16),
            pltpu.VMEM((PLANE - 1, 32, 1024), BF16),
            pltpu.VMEM((DEPTH, 8, 512), F32),
            pltpu.VMEM((DEPTH - 1, 8, 512), F32),
            pltpu.SemaphoreType.DMA,
            pltpu.SemaphoreType.DMA,
            pltpu.SemaphoreType.DMA,
            pltpu.SemaphoreType.DMA((2,)),
            pltpu.SemaphoreType.DMA((2,)),
            pltpu.SemaphoreType.DMA((PLANE - 1,)),
            pltpu.SemaphoreType.DMA((PLANE - 1,)),
            pltpu.SemaphoreType.DMA((DEPTH - 1,)),
            pltpu.SemaphoreType.DMA((DEPTH - 1,)),
        ],
        compiler_params=params(2),
    )(back, cell, tokens_in)


def on_device(tokens_in, queries, key_value, out_grad, cluster_of, slot_of):
    idx = jnp.stack([cluster_of.T.reshape(ROWS), slot_of.T.reshape(ROWS)])
    outgoing, labels, cell = pack(idx, queries, out_grad, key_value)
    qg, kv, live, lane = forward(outgoing, labels)
    back = attend(qg, kv, live, lane)
    return reduce(back, cell, tokens_in)


def solution(mesh):
    spec = P(("seq", "pair"), None)
    return jax.shard_map(
        on_device, mesh=mesh, in_specs=(spec,) * 6, out_specs=spec, check_vma=False
    )
```

time: 522 us -> 197 us (0.38)
  waiting for transfers between devices: 332 us -> 0 us
  Pallas kernels: 0 us -> 192 us
  local copies, waits for them, and re-layouts: 93.3 us -> 1.32 us
  starting transfers between devices: 38.6 us -> 0 us
  matrix products: 22.1 us -> 0 us
  other arithmetic: 19.2 us -> 1.33 us
  between operations: 13.7 us -> 0.03 us
    unnamed x3 -> x0, waiting for transfers between devices: 265 us -> none
    pallas_call x0 -> x4, Pallas kernels: none -> 192 us  [the longest x1 83.5 us: forward(): pl.pallas_call(forward_kernel, out_shape=(jax.ShapeDtypeStruct((CL_DEV, H...]
    all_to_all x3 -> x0, waiting for transfers between devices: 67.7 us -> none  [the longest x1 49.1 us: on_device(): lax.all_to_all(outgoing.reshape(groups, bound_rows, 4 * HD), 'seq', split...]
    scatter x3 -> x0, local copies, waits for them, and re-layouts: 55.5 us -> none  [the longest x1 28.6 us: on_device(): live_slot = jnp.zeros((slot_count,), jnp.bfloat16).at[target_safe].set(jn...]
    all_to_all x3 -> x0, starting transfers between devices: 38.4 us -> none  [the longest x1 15.4 us: on_device(): lax.all_to_all(labels.reshape(groups, bound_rows), 'seq', split_axis=0, c...]
    dot_general x25 -> x0, matrix products: 22.1 us -> none  [the longest x8 8.13 us: cluster_grad(): jnp.dot(score_grad, key_rows, preferred_element_type=jnp.float32)]
    gather x4 -> x0, local copies, waits for them, and re-layouts: 19.3 us -> none  [the longest x3 13.1 us: on_device(): slot_grads[jnp.minimum(target_safe, slot_count - 1)]]
    scatter x1 -> x0, other arithmetic: 11.5 us -> none  [on_device(): jnp.zeros((groups * bound_rows, 4 * HD), jnp.bfloat16).at[cell_index]]
  transfers between devices with their start and end apart: 5 -> 0, of which waited for: 3 -> 0; matrix products, arithmetic and copies ran while one was open for 8% -> 0% of each run, Pallas kernels for 0% -> 0%
where the time goes in v1:
time: 197 us; the launch traced here: 194 us
  Pallas kernels  192 us (97%)
    pallas_call x1, Pallas kernels, forward(): pl.pallas_call(forward_kernel, out_shape=(jax.ShapeDtypeStruct((CL_DEV, H...  83.5 us
    pallas_call x1, Pallas kernels, reduce(): pl.pallas_call(reduce_kernel, out_shape=jax.ShapeDtypeStruct((4, 1024), F...  51.7 us
    pallas_call x1, Pallas kernels, attend(): pl.pallas_call(attend_kernel, out_shape=jax.ShapeDtypeStruct((GROUPS, BOU...  46.1 us
    pallas_call x1, Pallas kernels, pack(): pl.pallas_call(pack_kernel, out_shape=(jax.ShapeDtypeStruct((GROUPS, BOUN...  10.5 us

profile of v1, /device:TPU:2, one launch (start us, length us, event | category | flops | bytes accessed | tf_op | source)
XLA Modules:
  0.0 194.5 jit_solution(9918843194480181549)
XLA Ops:
  0.0 1.3 pad_add_fusion.idx_ref
  1.3 10.5 %shard_map.64 = (bf16[128,32,256]{2,1,0:T(8,128)(2,1)}, s32[128,1,128]{2,1,0:T(1,128)}, s32[1,2048]{1,0:T(1,128)}) custom-call(s32[2,2048]{1,0:T(2,128)} %pad_add_fusion.idx_ref, bf16[128,1024]{1,0:T(8,128)(2,1)} %q_ref.1, bf16[128,1024]{1,0:T(8,128)(2,1)} %g_ref.1, bf16[128,128]{1,0:T(8,128)(2,1)} %kv_ref.1), custom_call_target="tpu_custom_call" | custom-call | tf_op jit(solution)/shard_map/pallas_call | solution.py:97
  11.8 83.5 %shard_map.65 = (bf16[8,512,128]{2,1,0:T(8,128)(2,1)}, bf16[8,512,128]{2,1,0:T(8,128)(2,1)}, f32[8,4,128]{2,1,0:T(4,128)}, s32[8,512]{1,0:T(8,128)}) custom-call(bf16[128,32,256]{2,1,0:T(8,128)(2,1)} %get-tuple-element.12.out_ref, s32[128,1,128]{2,1,0:T(1,128)} %get-tuple-element.13.lab_ref), custom_call_target="tpu_custom_call" | custom-call | tf_op jit(solution)/shard_map/pallas_call | solution.py:199
  95.3 46.1 %shard_map.66.back_ref = bf16[128,16,128]{2,1,0:T(8,128)(2,1)} custom-call(bf16[8,512,128]{2,1,0:T(8,128)(2,1)} %get-tuple-element.14.qg_ref, bf16[8,512,128]{2,1,0:T(8,128)(2,1)} %get-tuple-element.15.kv_ref, f32[8,4,128]{2,1,0:T(4,128)} %get-tuple-element.16.live_ref, s32[8,512]{1,0:T(8,128)} %get-tuple-element.17.lane_ref), custom_call_target="tpu_custom_call" | custom-call | tf_op jit(solution)/shard_map/pallas_call | solution.py:297
  141.4 51.7 %shard_map.67 = f32[4,1024]{1,0:T(4,128)} custom-call(bf16[128,16,128]{2,1,0:T(8,128)(2,1)} %shard_map.66.back_ref, s32[1,2048]{1,0:T(1,128)} %get-tuple-element.18.cell_ref, bf16[128,1024]{1,0:T(8,128)(2,1)} %x_ref.1), custom_call_target="tpu_custom_call" | custom-call | tf_op jit(solution)/shard_map/pallas_call | solution.py:420
  193.2 1.3 copy.8

commit v2 on v1

v2 whole, which is shorter than its diff:
```python
import functools

import jax
import jax.numpy as jnp
from jax import lax
from jax.experimental import pallas as pl
from jax.experimental.pallas import tpu as pltpu
from jax.sharding import PartitionSpec as P

H = 16
HD = 64
HALF = 512
CL_DEV = 8
TOK = 128
ROWS = TOK * H
SLOTS = CL_DEV * HALF
GROUPS = 128
BOUND = 32
PLANE = 16
DEPTH = 8
ORDER = [0, 1, 7, 2, 6, 3, 5, 4]
LAG = 2
MESH = pl.DeviceIdType.MESH
F32 = jnp.float32
BF16 = jnp.bfloat16
VMEM = pl.BlockSpec(memory_space=pltpu.VMEM)


def params(collective=None):
    if collective is None:
        return pltpu.CompilerParams(vmem_limit_bytes=56 * 2**20)
    return pltpu.CompilerParams(
        vmem_limit_bytes=56 * 2**20, collective_id=collective, has_side_effects=True
    )


def iota(shape, dim):
    return lax.broadcasted_iota(jnp.int32, shape, dim)


def one_hot(mask):
    return jnp.where(mask, 1.0, 0.0).astype(BF16)


def dot(a, b):
    return jnp.dot(a, b, preferred_element_type=F32)


def dot_t(a, b):
    return lax.dot_general(a, b, (((1,), (1,)), ((), ())), preferred_element_type=F32)


def t_dot(a, b):
    return lax.dot_general(a, b, (((0,), (0,)), ((), ())), preferred_element_type=F32)


def neighbours(seq, pair, with_other):
    yx, z = seq // DEPTH, lax.rem(seq, DEPTH)
    barrier = pltpu.get_barrier_semaphore()
    for i in range(1, DEPTH):
        to = yx * DEPTH + lax.rem(z + i, DEPTH)
        pl.semaphore_signal(barrier, inc=1, device_id=(to, pair), device_id_type=MESH)
    for m in range(1, PLANE):
        to = lax.rem(yx + m, PLANE) * DEPTH + z
        pl.semaphore_signal(barrier, inc=1, device_id=(to, pair), device_id_type=MESH)
    if with_other:
        pl.semaphore_signal(barrier, inc=1, device_id=(seq, 1 - pair), device_id_type=MESH)
    return barrier, DEPTH - 1 + PLANE - 1 + with_other


def forward_kernel(
    idx_ref, q_ref, g_ref, kvin_ref, qg_ref, kv_ref, live_ref, lane_ref, cell_ref,
    flat_ref, pick_ref, zsend_ref, zgot_ref, zkv_ref, zlab_ref, zlabgot_ref, group_ref, plab_ref,
    fwd_ref, rows_ref, total_ref, zsend_sem, zrecv_sem, lsend_sem, lrecv_sem, psend_sem, precv_sem,
):
    seq, pair = lax.axis_index("seq"), lax.axis_index("pair")
    yx, z = seq // DEPTH, lax.rem(seq, DEPTH)
    barrier, answers = neighbours(seq, pair, 0)

    cluster = idx_ref[0:1, :]
    slot = idx_ref[1:2, :]
    owner = lax.shift_right_logical(cluster, 3)
    local = (cluster & (CL_DEV - 1)) * HALF + (slot & (HALF - 1))
    pick_ref[...] = jnp.where(iota((GROUPS, ROWS), 0) == owner, 1.0, 0.0)
    before = one_hot(iota((TOK, TOK), 0) < iota((TOK, TOK), 1))
    base = jnp.zeros((GROUPS, 1), F32)
    ranks = []
    for h in range(H):
        pick = pick_ref[:, h * TOK : (h + 1) * TOK]
        count = dot(pick.astype(BF16), before) + base
        ranks.append(jnp.sum(pick * count, axis=0, keepdims=True))
        base = base + jnp.sum(pick, axis=1, keepdims=True)
    rank = jnp.concatenate(ranks, axis=1).astype(jnp.int32)
    cell_ref[0:1, :] = owner * BOUND + rank
    place = (owner & (DEPTH - 1)) * (PLANE * BOUND) + lax.shift_right_logical(owner, 3) * BOUND + rank
    in_row = jnp.where(iota((32, ROWS), 0) == lax.shift_right_logical(place, 7), 1.0, 0.0)
    in_lane = one_hot(iota((128, ROWS), 0) == (place & 127))
    token = iota((1, ROWS), 1) & (TOK - 1)
    parts = [lax.shift_right_logical(local, 6), local & 63, token]
    stacked = [(in_row * part.astype(F32)).astype(BF16) for part in parts] + [in_row.astype(BF16)]
    found = dot_t(jnp.concatenate(stacked, axis=0), in_lane)
    label = jnp.where(
        found[96:128] > 0.5, (found[0:32] * 64.0 + found[32:64]) * 128.0 + found[64:96], -1.0
    ).astype(jnp.int32)
    for i in range(DEPTH):
        zlab_ref[i] = label[4 * i : 4 * i + 4, :]
    for h in range(H):
        cut = slice(h * HD, (h + 1) * HD)
        flat_ref[h * TOK : (h + 1) * TOK, :] = jnp.concatenate([q_ref[:, cut], g_ref[:, cut]], axis=1)

    def z_copy(i, kind):
        to = lax.rem(z + i, DEPTH)
        source, target = (
            (zlab_ref.at[to], zlabgot_ref.at[i]),
            (kvin_ref, zkv_ref.at[i]),
            (zsend_ref.at[i], zgot_ref.at[i]),
        )[kind]
        return pltpu.make_async_remote_copy(
            src_ref=source, dst_ref=target, send_sem=zsend_sem.at[i, kind],
            recv_sem=zrecv_sem.at[i, kind], device_id=(yx * DEPTH + to, pair), device_id_type=MESH,
        )

    pl.semaphore_wait(barrier, answers)
    for kind in range(2):
        for i in ORDER[1:]:
            z_copy(i, kind).start()
    for i in ORDER[1:] + ORDER[:1]:
        to = lax.rem(z + i, DEPTH)
        hot = one_hot(iota((PLANE * BOUND, ROWS), 0) == place - to * (PLANE * BOUND))
        zsend_ref[i] = dot(hot, flat_ref[...]).astype(BF16)
        if i:
            z_copy(i, 2).start()
    zlabgot_ref[0] = zlab_ref[z]
    for i in ORDER[1:]:
        z_copy(i, 0).wait_recv()
    for i in range(DEPTH):
        for g in range(4):
            group_ref[g, i : i + 1, :] = zlabgot_ref[i, g : g + 1, :]

    def label_copy(m):
        to = lax.rem(yx + m, PLANE)
        return pltpu.make_async_remote_copy(
            src_ref=group_ref.at[to // 4], dst_ref=plab_ref.at[m], send_sem=lsend_sem.at[m],
            recv_sem=lrecv_sem.at[m], device_id=(to * DEPTH + z, pair), device_id_type=MESH,
        )

    for m in range(1, PLANE):
        label_copy(m).start()
    plab_ref[0] = group_ref[yx // 4]

    def row_copy(i, m):
        to = lax.rem(yx + m, PLANE)
        return pltpu.make_async_remote_copy(
            src_ref=fwd_ref.at[i, to], dst_ref=rows_ref.at[i, m], send_sem=psend_sem.at[i],
            recv_sem=precv_sem.at[i], device_id=(to * DEPTH + z, pair), device_id_type=MESH,
        )

    def all_rows(i):
        rest = pl.ds(1, PLANE - 1)
        return pltpu.make_async_remote_copy(
            src_ref=fwd_ref.at[i, rest], dst_ref=rows_ref.at[i, rest], send_sem=psend_sem.at[i],
            recv_sem=precv_sem.at[i], device_id=(seq, pair), device_id_type=MESH,
        )

    width = PLANE * BOUND

    def pass_on(i):
        if i:
            z_copy(i, 1).wait_recv()
            z_copy(i, 2).wait_recv()
        labels = jnp.concatenate([zlabgot_ref[i, g : g + 1, :] for g in range(4)], axis=1)
        hot = one_hot(iota((TOK, width), 0) == (labels & (TOK - 1)))
        pairs = t_dot(hot, zkv_ref[i] if i else kvin_ref[...]).astype(BF16)
        rows = zgot_ref[i] if i else zsend_ref[0]
        fwd_ref[i] = jnp.concatenate([rows, pairs], axis=1).reshape(PLANE, BOUND, 4 * HD)

        def send(m, carry):
            row_copy(i, m).start()
            return carry

        lax.fori_loop(1, PLANE, send, 0)
        rows_ref[i, 0] = fwd_ref[i, yx]

    def arrange(i, first, last):
        if first:
            for m in range(1, PLANE):
                label_copy(m).wait_recv()
        given = plab_ref[:, i, :]
        quarter = lax.rem(yx, 4)
        mine = given[:, 3 * BOUND :]
        for g in range(3):
            mine = jnp.where(quarter == g, given[:, g * BOUND : (g + 1) * BOUND], mine)
        lane = jnp.concatenate([mine[m : m + 1, :] for m in range(PLANE)], axis=1)
        lane = lax.shift_right_arithmetic(lane, 7)
        lane_ref[i : i + 1, :] = lane
        live = dot_t(
            one_hot(iota((SLOTS // 128, width), 0) == lax.shift_right_arithmetic(lane, 7)),
            one_hot(iota((128, width), 0) == (lane & 127)),
        )
        all_rows(i).wait_recv()

        def add(b, carry):
            hot = one_hot(iota((HALF, width), 0) == lane - b * HALF)
            term = dot(hot, rows_ref[i].reshape(width, 4 * HD))
            if first:
                total_ref[b] = term
            elif not last:
                total_ref[b] += term
            else:
                done = (total_ref[b] + term).astype(BF16)
                qg_ref[b] = done[:, : 2 * HD]
                kv_ref[b] = done[:, 2 * HD :]
            return carry

        lax.fori_loop(0, CL_DEV, add, 0)
        return live

    live = jnp.zeros((SLOTS // 128, 128), F32)
    for n in range(DEPTH + LAG):
        if n < DEPTH:
            pass_on(ORDER[n])
        if n >= LAG:
            live = live + arrange(ORDER[n - LAG], n == LAG, n == DEPTH + LAG - 1)
    for c in range(CL_DEV):
        live_ref[c] = live[4 * c : 4 * c + 4, :]
    for i in range(DEPTH):
        all_rows(i).wait_send()
        if i:
            for kind in range(3):
                z_copy(i, kind).wait_send()
    for m in range(1, PLANE):
        label_copy(m).wait_send()


def forward(idx, queries, out_grad, key_value):
    width = PLANE * BOUND
    return pl.pallas_call(
        forward_kernel,
        out_shape=(
            jax.ShapeDtypeStruct((CL_DEV, HALF, 2 * HD), BF16),
            jax.ShapeDtypeStruct((CL_DEV, HALF, 2 * HD), BF16),
            jax.ShapeDtypeStruct((CL_DEV, 4, 128), F32),
            jax.ShapeDtypeStruct((DEPTH, width), jnp.int32),
            jax.ShapeDtypeStruct((1, ROWS), jnp.int32),
        ),
        in_specs=[VMEM] * 4,
        out_specs=(VMEM,) * 5,
        scratch_shapes=[
            pltpu.VMEM((ROWS, 2 * HD), BF16),
            pltpu.VMEM((GROUPS, ROWS), F32),
            pltpu.VMEM((DEPTH, width, 2 * HD), BF16),
            pltpu.VMEM((DEPTH, width, 2 * HD), BF16),
            pltpu.VMEM((DEPTH, TOK, 2 * HD), BF16),
            pltpu.VMEM((DEPTH, 4, 128), jnp.int32),
            pltpu.VMEM((DEPTH, 4, 128), jnp.int32),
            pltpu.VMEM((4, DEPTH, 128), jnp.int32),
            pltpu.VMEM((PLANE, DEPTH, 128), jnp.int32),
            pltpu.VMEM((DEPTH, PLANE, BOUND, 4 * HD), BF16),
            pltpu.VMEM((DEPTH, PLANE, BOUND, 4 * HD), BF16),
            pltpu.VMEM((CL_DEV, HALF, 4 * HD), F32),
            pltpu.SemaphoreType.DMA((DEPTH, 3)),
            pltpu.SemaphoreType.DMA((DEPTH, 3)),
            pltpu.SemaphoreType.DMA((PLANE,)),
            pltpu.SemaphoreType.DMA((PLANE,)),
            pltpu.SemaphoreType.DMA((DEPTH,)),
            pltpu.SemaphoreType.DMA((DEPTH,)),
        ],
        compiler_params=params(0),
    )(idx, queries, out_grad, key_value)


def backward_kernel(
    qg_ref, kv_ref, live_ref, lane_ref, cell_ref, x_ref, out_ref,
    kv2_ref, live2_ref, s_ref, d_ref, w_ref, grads_ref, back_ref, zback_ref, got_ref, hot_ref,
    xp_ref, g_ref, xo_ref, go_ref, part_ref, plane_ref, line_ref, lined_ref,
    ksend_sem, krecv_sem, bsend_sem, brecv_sem, rsend_sem, rrecv_sem, psend_sem, precv_sem,
    ysend_sem, yrecv_sem, zsend_sem, zrecv_sem,
):
    seq, pair = lax.axis_index("seq"), lax.axis_index("pair")
    other = (seq, 1 - pair)
    yx, z = seq // DEPTH, lax.rem(seq, DEPTH)
    barrier, answers = neighbours(seq, pair, 1)
    pl.semaphore_wait(barrier, answers)

    def key_copy(c):
        return pltpu.make_async_remote_copy(
            src_ref=kv_ref.at[c], dst_ref=kv2_ref.at[c], send_sem=ksend_sem.at[c],
            recv_sem=krecv_sem.at[c], device_id=other, device_id_type=MESH,
        )

    live_copy = pltpu.make_async_remote_copy(
        src_ref=live_ref, dst_ref=live2_ref, send_sem=ksend_sem.at[CL_DEV],
        recv_sem=krecv_sem.at[CL_DEV], device_id=other, device_id_type=MESH,
    )
    live_copy.start()
    for c in range(CL_DEV):
        key_copy(c).start()
    position = iota((1024, 512), 1)
    for p in range(2):
        column = lax.shift_right_logical(position, 2) * 8 + 4 * p + (position & 3)
        xp_ref[p] = dot(x_ref[...], one_hot(iota((1024, 512), 0) == column)).astype(BF16)
    x_copy = pltpu.make_async_remote_copy(
        src_ref=xp_ref.at[1 - pair], dst_ref=xo_ref, send_sem=psend_sem.at[0],
        recv_sem=precv_sem.at[0], device_id=other, device_id_type=MESH,
    )
    x_copy.start()
    live_copy.wait()

    for c in range(CL_DEV):
        key_copy(c).wait()
        queries = qg_ref[c, :, :HD] * BF16(HD**-0.5)
        grads = qg_ref[c, :, HD:]
        keys = jnp.concatenate([kv_ref[c, :, :HD], kv2_ref[c, :, :HD]], axis=0)
        values = jnp.concatenate([kv_ref[c, :, HD:], kv2_ref[c, :, HD:]], axis=0)
        alive = jnp.concatenate(
            [ref[c, r : r + 1, :] for ref in (live_ref, live2_ref) for r in range(4)], axis=1
        )
        bias = jnp.where(alive > 0.5, 0.0, -1e30)
        s_ref[...] = dot_t(queries, keys)
        d_ref[...] = dot_t(grads, values)

        def rows(r, carry, bias=bias):
            at = pl.ds(pl.multiple_of(r * 32, 32), 32)
            scores = s_ref[at, :] + bias
            weights = jnp.exp(scores - jnp.max(scores, axis=1, keepdims=True))
            inverse = 1.0 / jnp.sum(weights, axis=1, keepdims=True)
            prob_grad = d_ref[at, :]
            row_dot = jnp.sum(weights * prob_grad, axis=1, keepdims=True) * inverse
            w_ref[at, :] = (
                weights * (prob_grad - row_dot) * (inverse * (HD**-0.5))
            ).astype(BF16)
            return carry

        lax.fori_loop(0, HALF // 32, rows, 0)
        place = slice((c % 2) * HALF, (c % 2 + 1) * HALF)
        column = slice((c // 2) * HD, (c // 2 + 1) * HD)
        grads_ref[place, column] = dot(w_ref[...], keys).astype(BF16)

    def back_copy(i):
        to = lax.rem(z + (DEPTH - i), DEPTH)
        return pltpu.make_async_remote_copy(
            src_ref=back_ref.at[i], dst_ref=zback_ref.at[i], send_sem=bsend_sem.at[i],
            recv_sem=brecv_sem.at[i], device_id=(yx * DEPTH + to, pair), device_id_type=MESH,
        )

    width = PLANE * BOUND
    for i in ORDER[1:] + ORDER[:1]:
        labels = jnp.broadcast_to(lane_ref[i : i + 1, :], (128, width)).T
        low = labels & 1023
        hot = jnp.concatenate(
            [one_hot(low == iota((width, 128), 1) + 128 * b) for b in range(8)], axis=1
        )
        found = dot(hot, grads_ref[...])
        high = lax.shift_right_arithmetic(labels[:, :HD], 10)
        row = jnp.zeros((width, HD), F32)
        for a in range(4):
            row = row + jnp.where(high == a, found[:, a * HD : (a + 1) * HD], 0.0)
        row = row.reshape(PLANE, BOUND, HD)
        row = jnp.concatenate([row[:, : BOUND // 2], row[:, BOUND // 2 :]], axis=2).astype(BF16)
        if i:
            back_ref[i] = row
            back_copy(i).start()
        else:
            zback_ref[0] = row

    def return_copy(i, m):
        to = lax.rem(yx + (PLANE - m), PLANE)
        return pltpu.make_async_remote_copy(
            src_ref=zback_ref.at[i, m], dst_ref=got_ref.at[i, m], send_sem=rsend_sem.at[i],
            recv_sem=rrecv_sem.at[i], device_id=(to * DEPTH + z, pair), device_id_type=MESH,
        )

    def all_returns(i):
        rest = pl.ds(1, PLANE - 1)
        return pltpu.make_async_remote_copy(
            src_ref=zback_ref.at[i, rest], dst_ref=got_ref.at[i, rest], send_sem=rsend_sem.at[i],
            recv_sem=rrecv_sem.at[i], device_id=other, device_id_type=MESH,
        )

    for n, i in enumerate(ORDER):
        if i:
            back_copy(i).wait_recv()

        def send(m, carry, i=i):
            return_copy(i, m).start()
            return carry

        lax.fori_loop(1, PLANE, send, 0)
        got_ref[i, 0] = zback_ref[i, 0]
        for h in (2 * n, 2 * n + 1):
            cell = cell_ref[0:1, h * TOK : (h + 1) * TOK]
            line = lax.shift_right_logical(cell, 5) + (DEPTH - z)
            plane = lax.shift_right_logical(cell, 8) + (PLANE - yx)
            target = (line & (DEPTH - 1)) * (PLANE * BOUND // 2) + (plane & (PLANE - 1)) * (BOUND // 2)
            target = jnp.broadcast_to(target + (cell & (BOUND // 2 - 1)), (TOK, TOK)).T
            for b in range(16):
                hot_ref[h * TOK : (h + 1) * TOK, b * 128 : (b + 1) * 128] = one_hot(
                    target == iota((TOK, 128), 1) + 128 * b
                )
    for i in ORDER:
        all_returns(i).wait_recv()
    got = got_ref[...].reshape(GROUPS * BOUND // 2, 2 * HD)
    for h in range(0, H, 2):
        found = dot(hot_ref[h * TOK : (h + 2) * TOK, :], got)
        pieces = []
        for e in range(2):
            cell = cell_ref[0:1, (h + e) * TOK : (h + e + 1) * TOK]
            upper = (jnp.broadcast_to(cell, (TOK, TOK)).T[:, :HD] & (BOUND // 2)) > 0
            piece = found[e * TOK : (e + 1) * TOK]
            pieces.append(jnp.where(upper, piece[:, HD:], piece[:, :HD]))
        g_ref[:, h * HD : (h + 2) * HD] = jnp.concatenate(pieces, axis=1).astype(BF16)
    g_copy = pltpu.make_async_remote_copy(
        src_ref=g_ref, dst_ref=go_ref, send_sem=psend_sem.at[1], recv_sem=precv_sem.at[1],
        device_id=other, device_id_type=MESH,
    )
    g_copy.start()
    x_copy.wait()
    g_copy.wait()
    left, right = xp_ref[pair], xo_ref[...]
    for b in range(4):
        cut = slice(b * 128, (b + 1) * 128)
        term = t_dot(left[:, cut], g_ref[...]) + t_dot(right[:, cut], go_ref[...])
        part_ref[b * 4 : (b + 1) * 4] = term.astype(BF16).reshape(4, 32, 1024)

    def plane_copy(i):
        to = lax.rem(yx + i, PLANE)
        return pltpu.make_async_remote_copy(
            src_ref=part_ref.at[to], dst_ref=plane_ref.at[i - 1], send_sem=ysend_sem.at[i - 1],
            recv_sem=yrecv_sem.at[i - 1], device_id=(to * DEPTH + z, pair), device_id_type=MESH,
        )

    for i in range(1, PLANE):
        plane_copy(i).start()
    total = part_ref[yx].astype(F32)
    for i in range(1, PLANE):
        plane_copy(i).wait_recv()
        total = total + plane_ref[i - 1].astype(F32)
    for i in range(DEPTH):
        rows = total[4 * i : 4 * i + 4, :]
        line_ref[i] = jnp.concatenate([rows[:, :512], rows[:, 512:]], axis=0)

    def line_copy(i):
        to = lax.rem(z + i, DEPTH)
        return pltpu.make_async_remote_copy(
            src_ref=line_ref.at[to], dst_ref=lined_ref.at[i - 1], send_sem=zsend_sem.at[i - 1],
            recv_sem=zrecv_sem.at[i - 1], device_id=(yx * DEPTH + to, pair), device_id_type=MESH,
        )

    for i in range(1, DEPTH):
        line_copy(i).start()
    result = line_ref[z]
    for i in range(1, DEPTH):
        line_copy(i).wait_recv()
        result = result + lined_ref[i - 1]
    out_ref[...] = jnp.concatenate([result[:4], result[4:]], axis=1)
    for i in range(1, DEPTH):
        back_copy(i).wait_send()
    for i in range(DEPTH):
        all_returns(i).wait_send()
    for i in range(1, PLANE):
        plane_copy(i).wait_send()
    for i in range(1, DEPTH):
        line_copy(i).wait_send()


def backward(qg, kv, live, lane, cell, tokens_in):
    return pl.pallas_call(
        backward_kernel,
        out_shape=jax.ShapeDtypeStruct((4, 1024), F32),
        in_specs=[VMEM] * 6,
        out_specs=VMEM,
        scratch_shapes=[
            pltpu.VMEM((CL_DEV, HALF, 2 * HD), BF16),
            pltpu.VMEM((CL_DEV, 4, 128), F32),
            pltpu.VMEM((HALF, 2 * HALF), F32),
            pltpu.VMEM((HALF, 2 * HALF), F32),
            pltpu.VMEM((HALF, 2 * HALF), BF16),
            pltpu.VMEM((2 * HALF, 4 * HD), BF16),
            pltpu.VMEM((DEPTH, PLANE, BOUND // 2, 2 * HD), BF16),
            pltpu.VMEM((DEPTH, PLANE, BOUND // 2, 2 * HD), BF16),
            pltpu.VMEM((DEPTH, PLANE, BOUND // 2, 2 * HD), BF16),
            pltpu.VMEM((ROWS, GROUPS * BOUND // 2), BF16),
            pltpu.VMEM((2, TOK, 512), BF16),
            pltpu.VMEM((TOK, 1024), BF16),
            pltpu.VMEM((TOK, 512), BF16),
            pltpu.VMEM((TOK, 1024), BF16),
            pltpu.VMEM((PLANE, 32, 1024), BF16),
            pltpu.VMEM((PLANE - 1, 32, 1024), BF16),
            pltpu.VMEM((DEPTH, 8, 512), F32),
            pltpu.VMEM((DEPTH - 1, 8, 512), F32),
            pltpu.SemaphoreType.DMA((CL_DEV + 1,)),
            pltpu.SemaphoreType.DMA((CL_DEV + 1,)),
            pltpu.SemaphoreType.DMA((DEPTH,)),
            pltpu.SemaphoreType.DMA((DEPTH,)),
            pltpu.SemaphoreType.DMA((DEPTH,)),
            pltpu.SemaphoreType.DMA((DEPTH,)),
            pltpu.SemaphoreType.DMA((2,)),
            pltpu.SemaphoreType.DMA((2,)),
            pltpu.SemaphoreType.DMA((PLANE - 1,)),
            pltpu.SemaphoreType.DMA((PLANE - 1,)),
            pltpu.SemaphoreType.DMA((DEPTH - 1,)),
            pltpu.SemaphoreType.DMA((DEPTH - 1,)),
        ],
        compiler_params=params(1),
    )(qg, kv, live, lane, cell, tokens_in)


def on_device(tokens_in, queries, key_value, out_grad, cluster_of, slot_of):
    idx = jnp.stack([cluster_of.T.reshape(ROWS), slot_of.T.reshape(ROWS)])
    qg, kv, live, lane, cell = forward(idx, queries, out_grad, key_value)
    return backward(qg, kv, live, lane, cell, tokens_in)


def solution(mesh):
    spec = P(("seq", "pair"), None)
    return jax.shard_map(
        on_device, mesh=mesh, in_specs=(spec,) * 6, out_specs=spec, check_vma=False
    )
```

time: 197 us -> 155 us (0.79)
  Pallas kernels: 192 us -> 150 us
    pallas_call x1, Pallas kernels: 83.5 us -> 55.8 us  [forward(): pl.pallas_call(forward_kernel, out_shape=(jax.ShapeDtypeStruct((CL_DEV, H...]
    pallas_call x3 -> x1, Pallas kernels: 108 us -> 94.1 us  [backward(): pl.pallas_call(backward_kernel, out_shape=jax.ShapeDtypeStruct((4, 1024),...]
where the time goes in v2:
time: 155 us; the launch traced here: 152 us
  Pallas kernels  150 us (97%)
    pallas_call x1, Pallas kernels, backward(): pl.pallas_call(backward_kernel, out_shape=jax.ShapeDtypeStruct((4, 1024),...  94.1 us
    pallas_call x1, Pallas kernels, forward(): pl.pallas_call(forward_kernel, out_shape=(jax.ShapeDtypeStruct((CL_DEV, H...  55.8 us

profile of v2, /device:TPU:2, one launch (start us, length us, event | category | flops | bytes accessed | tf_op | source)
XLA Modules:
  0.0 152.5 jit_solution(6703524258911835266)
XLA Ops:
  0.0 1.3 pad_add_fusion.idx_ref
  1.3 55.8 %shard_map.64 = (bf16[8,512,128]{2,1,0:T(8,128)(2,1)}, bf16[8,512,128]{2,1,0:T(8,128)(2,1)}, f32[8,4,128]{2,1,0:T(4,128)}, s32[8,512]{1,0:T(8,128)}, s32[1,2048]{1,0:T(1,128)}) custom-call(s32[2,2048]{1,0:T(2,128)} %pad_add_fusion.idx_ref, bf16[128,1024]{1,0:T(8,128)(2,1)} %q_ref.1, bf16[128,1024]{1,0:T(8,128)(2,1)} %g_ref.1, bf16[128,128]{1,0:T(8,128)(2,1)} %kvin_ref.1), custom_call_target="tpu_custom_call" | custom-call | tf_op jit(solution)/shard_map/pallas_call | solution.py:237
  57.1 94.1 %shard_map.65 = f32[4,1024]{1,0:T(4,128)} custom-call(bf16[8,512,128]{2,1,0:T(8,128)(2,1)} %get-tuple-element.10.qg_ref, bf16[8,512,128]{2,1,0:T(8,128)(2,1)} %get-tuple-element.11.kv_ref, f32[8,4,128]{2,1,0:T(4,128)} %get-tuple-element.12.live_ref, s32[8,512]{1,0:T(8,128)} %get-tuple-element.13.lane_ref, s32[1,2048]{1,0:T(1,128)} %get-tuple-element.14.cell_ref, ...), custom_call_target="tpu_custom_call" | custom-call | tf_op jit(solution)/shard_map/pallas_call | solution.py:467
  151.2 1.3 copy.8
